TPU v7x, 32 devices: a whole 2x2x4 slice. The times are simulated.
32 devices in a mesh: edge: 16 (over z, y, x), rep: 2 (over core).
Axes of the slice: x: 2, y: 2, z: 4, core: 2. Of those that a mesh axis runs over, the one named last changes fastest.
Arguments:
- nodes: bfloat16 [64, 131072], P(None, ('edge', 'rep')), may hold values from -6 to 6
- edges: bfloat16 [64, 524288], P(None, ('edge', 'rep')), may hold values from -6 to 6
- target: bfloat16 [64, 131072], P(None, ('edge', 'rep')), may hold values from -6 to 6
- senders: int32 [524288], P(('edge', 'rep')), may hold values from 0 to 4095
- receivers: int32 [524288], P(('edge', 'rep')), may hold values from 0 to 4095
- counts: int32 [512], P(('edge', 'rep')), may hold values from 1 to 1024, as said below
- levels: int32 [131072], P(('edge', 'rep')), may hold values from 0 to 3
- land: int32 [131072], P(('edge', 'rep')), may hold values 0 or 1
- channel_mask: int32 [4, 64], replicated, may hold values 0 or 1
- edge_in: bfloat16 [192, 64], replicated, may hold values from -0.4375 to 0.4375
- edge_in_bias: bfloat16 [64], replicated, may hold values from -3 to 3
- edge_out: bfloat16 [64, 64], replicated, may hold values from -0.75 to 0.75
- edge_out_bias: bfloat16 [64], replicated, may hold values from -3 to 3
- edge_gain: bfloat16 [64], replicated, may hold values from 0.25 to 1.75
- edge_shift: bfloat16 [64], replicated, may hold values from -3 to 3
- node_in: bfloat16 [128, 64], replicated, may hold values from -0.5 to 0.5
- node_in_bias: bfloat16 [64], replicated, may hold values from -3 to 3
- node_out: bfloat16 [64, 64], replicated, may hold values from -0.75 to 0.75
- node_out_bias: bfloat16 [64], replicated, may hold values from -3 to 3
- node_gain: bfloat16 [64], replicated, may hold values from 0.25 to 1.75
- node_shift: bfloat16 [64], replicated, may hold values from -3 to 3
Outputs:
- new_nodes: bfloat16 [64, 131072], P(None, ('edge', 'rep'))
- node_grad: bfloat16 [64, 131072], P(None, ('edge', 'rep'))
- edge_grad: bfloat16 [64, 524288], P(None, ('edge', 'rep'))
- edge_in_grad: float32 [192, 64], replicated
- edge_in_bias_grad: float32 [64], replicated
- edge_out_grad: float32 [64, 64], replicated
- edge_out_bias_grad: float32 [64], replicated
- edge_gain_grad: float32 [64], replicated
- edge_shift_grad: float32 [64], replicated
- node_in_grad: float32 [128, 64], replicated
- node_in_bias_grad: float32 [64], replicated
- node_out_grad: float32 [64, 64], replicated
- node_out_bias_grad: float32 [64], replicated
- node_gain_grad: float32 [64], replicated
- node_shift_grad: float32 [64], replicated
Inputs may be any that keep to these rules, and one draw needn't show every extreme that they name: `counts`: in every draw some owner gets 1024 live slots from every sender block of its region, and another gets exactly 1 from every one.
All inputs are finite; a program needn't handle non-finite values. No bound on the sum of `land` on one device may be relied on, other than what follows from the above.
Results may differ from a plain program's by a relative error of at most 0.0081.
Values may be sent and summed in bfloat16 or wider, within the bound.
A program may use at most 128 MiB of HBM per device.

v0:
```python
import functools

import jax
import jax.numpy as jnp
from jax import lax
from jax.experimental import pallas as pl
from jax.experimental.pallas import tpu as pltpu
from jax.sharding import PartitionSpec as P

NORM_EPS = 1e-05
F32 = jnp.float32
BF16 = jnp.bfloat16
LOW = 256
VMEM_LIMIT = 60 * 2**20
PLANES = 4
EDGE_PLAN = {
    ('table', 1): ((1, 0), (1, 1), (1, 2), (1, 3)),
    ('table', 2): ((2, 0), (2, 1), (2, 2), (2, 3)),
    ('table', 3): ((3, 0),),
    ('edges', 0): ((3, 1),),
    ('edges', 2): ((3, 2),),
    ('edges', 5): ((3, 3),),
}
BACK_PLAN = {
    ('table', 1): ((1, 0), (1, 1), (1, 2), (1, 3)),
    ('table', 2): ((2, 0), (2, 1), (2, 2), (2, 3)),
    ('table', 3): ((3, 0),),
    ('sums', 1): ((3, 1),),
    ('sums', 7): ((3, 2),),
    ('finish', 2): ((3, 3),),
}
MESH = pl.DeviceIdType.MESH

EB1, EB2, EG, EH, NB1, NB2, NG, NH, CM = 0, 1, 2, 3, 4, 5, 6, 7, 8


def dot(a, b):
    return jnp.dot(a, b, preferred_element_type=F32)


def dot_tn(a, b):
    return lax.dot_general(a, b, (((0,), (0,)), ((), ())), preferred_element_type=F32)


def dot_nt(a, b):
    return lax.dot_general(a, b, (((1,), (1,)), ((), ())), preferred_element_type=F32)


def one_hot_low(ids):
    low = ids & (LOW - 1)
    rows = lax.broadcasted_iota(jnp.int32, (LOW, ids.shape[1]), 0)
    return (rows == low).astype(F32).astype(BF16)


def high_of(ids, rows):
    high = ids >> (LOW.bit_length() - 1)
    return jnp.broadcast_to(high.astype(F32).astype(BF16), (rows, ids.shape[1]))


def stack_table(table_ref, value):
    rows = value.shape[0]
    for h in range(value.shape[1] // LOW):
        table_ref[h * rows : (h + 1) * rows, :] = value[:, h * LOW : (h + 1) * LOW]


def gather_columns(table, ids, rows):
    picked = dot(table, one_hot_low(ids)).astype(BF16)
    high = high_of(ids, rows)
    out = picked[:rows]
    for h in range(1, table.shape[0] // rows):
        out = jnp.where(high == BF16(h), picked[h * rows : (h + 1) * rows], out)
    return out


def scatter_columns(values, ids, count):
    rows = values.shape[0]
    high = high_of(ids, rows)
    zero = jnp.zeros_like(values)
    spread = jnp.concatenate(
        [jnp.where(high == BF16(h), values, zero) for h in range(count // LOW)], axis=0
    )
    return dot_nt(spread, one_hot_low(ids))


def column(cols, index):
    return cols[:, index : index + 1]


def mean_rows(v):
    return jnp.mean(v, axis=0, keepdims=True)


def lane_sums(v):
    out = v[:, :128]
    for k in range(1, v.shape[1] // 128):
        out = out + v[:, k * 128 : (k + 1) * 128]
    return out


def branch_forward(w1t, w2t, b1, b2, stacked):
    pre = dot(w1t, stacked) + b1
    hidden = (pre * (1.0 / (1.0 + jnp.exp(-pre)))).astype(BF16)
    outer = dot(w2t, hidden) + b2
    shifted = outer - mean_rows(outer)
    inverse = lax.rsqrt(mean_rows(shifted * shifted) + NORM_EPS)
    return pre, shifted * inverse, inverse


def branch_backward(w2, gain, grad, pre, normal, inverse):
    q = grad * gain
    outer_grad = (
        inverse * (q - mean_rows(q) - normal * mean_rows(q * normal))
    ).astype(BF16)
    s = 1.0 / (1.0 + jnp.exp(-pre))
    pre_grad = (dot(w2, outer_grad) * (s * (1.0 + pre * (1.0 - s)))).astype(BF16)
    return outer_grad, pre_grad, (pre * s).astype(BF16)


def split_dot(low, wide):
    top = wide.astype(BF16)
    rest = (wide - top.astype(F32)).astype(BF16)
    return dot(low, top) + dot(low, rest)


def layer_kernel(
    levels_count, reps,
    counts, nodes, edges_in, target_in, senders, receivers, levels, land, masks, ew1t, ew2, nw1t,
    nw2,
    eb1, eb2, eg, eh, nb1, nb2, ng, nh,
    new_nodes, node_grad, edge_grad, summed,
    edges, target, new_hold, node_hold, in_sem, out_sem, grad_sem, tabs, send_a, recv_s, recv_e, mine, ids_tab, count_send, count_recv, pre_s, normal_s,
    inverse_s, recv_c, send_d, recv_d, total, part, grads, sums, pieces, ew1, ew2t, nw1, nw2t, cols,
    tab_send, tab_recv, ids_send, ids_recv, a_send, a_recv, b_send, b_recv, count_out, count_in,
    piece_send, piece_recv, sum_send, sum_recv,
):
    rows, count = nodes.shape
    owners, cap = senders.shape[0], senders.shape[2]
    ring = owners // PLANES
    high_count = count // LOW
    chunks = tab_recv.shape[2]
    chunk = tabs.shape[2] // chunks
    e, rep = lax.axis_index("edge"), lax.axis_index("rep")
    z, r = e // ring, e % ring
    me, devices = e * reps + rep, owners * reps
    upper = z // 2

    def plane_at(k):
        low = z + upper * (3 - 2 * z)
        turned = lax.rem(k + 1, 3) * (1 - k // 3) + 3 * (k // 3)
        place = k * (1 - low) + turned * low
        return place + upper * (3 - 2 * place)

    order = tuple(plane_at(k) for k in range(PLANES))
    middle = lax.rem(z, 3) != 0
    toward = 3 - 2 * z

    def at(plane, place):
        return (plane * ring + place, rep)

    def remote(src, dst, send, recv, device):
        return pltpu.make_async_remote_copy(
            src, dst, send, recv, device_id=device, device_id_type=MESH
        )

    def loop(low, high, body):
        def step(i, carry):
            body(i)
            return carry

        lax.fori_loop(low, high, step, 0)

    def others(body):
        def one(t):
            d = lax.rem(me + t, devices)
            body(d, (d // reps, lax.rem(d, reps)))

        loop(1, devices, one)

    load_edges = pltpu.make_async_copy(edges_in, edges, in_sem.at[0])
    load_target = pltpu.make_async_copy(target_in, target, in_sem.at[1])
    load_edges.start()
    load_target.start()

    barrier = pltpu.get_barrier_semaphore()
    others(
        lambda d, device: pl.semaphore_signal(
            barrier, inc=1, device_id=device, device_id_type=MESH
        )
    )

    stack_table(tabs.at[0, z], nodes[...])
    pl.semaphore_wait(barrier, devices - 1)

    def part_of(phase, plane, c):
        return tabs.at[phase, plane, pl.ds(c * chunk, chunk)]

    def table_copy(phase, plane, c, lane, to):
        return remote(
            part_of(phase, plane, c), part_of(phase, plane, c),
            tab_send.at[phase, lane, c], tab_recv.at[phase, plane, c], at(to, r),
        )

    def await_table(phase, plane, c):
        table_copy(phase, plane, c, 0, z).wait_recv()

    def send_own(phase, c):
        @pl.when(z < PLANES - 1)
        def _():
            table_copy(phase, z, c, 0, z + 1).start()

        @pl.when(z > 0)
        def _():
            table_copy(phase, z, c, 1, z - 1).start()

    def relay(phase, slot):
        @pl.when(middle)
        def _():
            for c in range(chunks):
                if slot == 0:
                    await_table(phase, z - toward, c)
                    table_copy(phase, z - toward, c, 2, z + toward).start()
                    await_table(phase, z + toward, c)
                    table_copy(phase, z + toward, c, 3, z - toward).start()
                else:
                    await_table(phase, z + 2 * toward, c)
                    table_copy(phase, z + 2 * toward, c, 4, z - toward).start()

    def end_wait(phase, k):
        @pl.when(jnp.logical_not(middle))
        def _():
            for c in range(chunks):
                await_table(phase, order[k], c)

    def drain_tables(phase):
        for c in range(chunks):
            @pl.when(z < PLANES - 1)
            def _():
                table_copy(phase, z, c, 0, z + 1).wait_send()

            @pl.when(z > 0)
            def _():
                table_copy(phase, z, c, 1, z - 1).wait_send()

            @pl.when(middle)
            def _():
                table_copy(phase, z - toward, c, 2, z + toward).wait_send()
                table_copy(phase, z + toward, c, 3, z - toward).wait_send()
                table_copy(phase, z + 2 * toward, c, 4, z - toward).wait_send()

    def ids_copy(phase, ids, k):
        plane = lax.rem(z + k, PLANES)
        return remote(
            ids.at[pl.ds(plane * ring, ring)], ids_tab.at[phase, pl.ds(z * ring, ring)],
            ids_send.at[phase, plane], ids_recv.at[phase, z], at(plane, r),
        )

    def ids_arrival(phase, plane):
        rows_of = ids_tab.at[phase, pl.ds(plane * ring, ring)]
        return remote(
            rows_of, rows_of, ids_send.at[phase, plane], ids_recv.at[phase, plane], at(plane, r)
        )

    def plane_copy(phase, plane, to, into):
        return remote(
            send_a.at[plane * ring + to], into.at[plane * ring + r],
            a_send.at[phase, plane * ring + to], a_recv.at[phase, plane * ring + r], at(z, to),
        )

    def plane_arrival(phase, j, into):
        return remote(
            send_a.at[j], into.at[j], a_send.at[phase, j], a_recv.at[phase, j], at(z, r)
        )

    def hand_over(phase, plane, to, t, got, into):
        @pl.when(t < ring)
        def _():
            send_a[plane * ring + to] = got
            plane_copy(phase, plane, to, into).start()

        @pl.when(t == ring)
        def _():
            into[plane * ring + r] = got

    def gather_step(phase, k, into):
        plane = plane_at(k)

        def two(ts):
            tos = [lax.rem(r + t + 1, ring) for t in ts]
            got = gather_columns(
                tabs[phase, plane],
                side_by_side([ids_tab[phase, plane * ring + to] for to in tos]), rows,
            )
            for i, (t, to) in enumerate(zip(ts, tos)):
                hand_over(phase, plane, to, t + 1, got[:, i * cap : (i + 1) * cap], into)

        in_pairs(two)

    def drain_planes(phase, into):
        for plane in range(PLANES):
            loop(1, ring, lambda t: plane_copy(phase, plane, lax.rem(r + t, ring), into).wait_send())

    def lanes(j):
        return pl.ds(pl.multiple_of(j * cap, cap), cap)

    def edges_copy(j):
        return remote(
            edges.at[:, lanes(j)], recv_e.at[e], b_send.at[0, j], b_recv.at[0, e], (j, rep)
        )

    def edges_arrival(a):
        return remote(
            edges.at[:, lanes(a)], recv_e.at[a], b_send.at[0, a], b_recv.at[0, a], (e, rep)
        )

    def count_copy(j):
        return remote(
            count_send.at[j], count_recv.at[e], count_out.at[j], count_in.at[e], (j, rep)
        )

    def count_arrival(a):
        return remote(
            count_send.at[a], count_recv.at[a], count_out.at[a], count_in.at[a], (e, rep)
        )

    def back_copy(a):
        return remote(
            send_d.at[a], recv_d.at[e], b_send.at[1, a], b_recv.at[1, e], (a, rep)
        )

    def back_arrival(j):
        return remote(
            send_d.at[j], recv_d.at[j], b_send.at[1, j], b_recv.at[1, j], (e, rep)
        )

    def peers(body):
        loop(1, owners, lambda t: body(lax.rem(e + t, owners)))

    def in_pairs(body):
        loop(0, ring // 2, lambda h: body((2 * h, 2 * h + 1)))

    def steps(body):
        loop(0, PLANES, body)

    def step_in_pairs(body, before):
        def one(i):
            k, h = i // (ring // 2), lax.rem(i, ring // 2)
            ts = (2 * h, 2 * h + 1)
            before(i)
            body(plane_at(k), ts, [k + t > 0 for t in ts])

        loop(0, PLANES * (ring // 2), one)

    def side_by_side(blocks):
        return jnp.concatenate(blocks, axis=1)

    def send_edges(k, low, high):
        loop(low, high, lambda t: edges_copy(order[k] * ring + lax.rem(r + t, ring)).start())

    place = lax.broadcasted_iota(jnp.int32, (1, cap), 1)

    def live_here(a):
        line = count_recv[a]
        wide = jnp.concatenate([line] * (cap // line.shape[1]), axis=1)
        return (place < wide).astype(F32)

    def edge_forward(a):
        own = recv_e[a]
        pre, normal, inverse = branch_forward(
            ew1t[...], ew2t[...], column(cols, EB1), column(cols, EB2),
            jnp.concatenate([own, recv_s[a], mine[a]], axis=0),
        )
        pre_s[a] = pre
        normal_s[a] = normal
        inverse_s[a] = inverse
        updated = own.astype(F32) + (normal * column(cols, EG) + column(cols, EH))
        return (updated * live_here(a)).astype(BF16)

    def forward_steps():
        def two(plane, ts, remotes):
            froms = [plane * ring + lax.rem(r + ring - t, ring) for t in ts]
            for t, a, there in zip(ts, froms, remotes):
                @pl.when(t > 0)
                def _():
                    plane_arrival(0, a, recv_s).wait_recv()

                @pl.when(there)
                def _():
                    count_arrival(a).wait_recv()
                    edges_arrival(a).wait_recv()

            total[...] += scatter_columns(
                side_by_side([edge_forward(a) for a in froms]),
                side_by_side([receivers[a] for a in froms]), count,
            )

        turns = PLANES * (ring // 2)
        step_in_pairs(two, lambda i: emit_at(EDGE_PLAN, "edges", i, turns, send_edges))

    def edge_backward(a, got):
        grad = got.astype(F32) * live_here(a)
        normal = normal_s[a]
        outer_grad, pre_grad, hidden = branch_backward(
            ew2[...], column(cols, EG), grad, pre_s[a], normal, inverse_s[a]
        )
        grads[...] += dot_nt(
            jnp.concatenate([recv_e[a], recv_s[a], mine[a], hidden], axis=0),
            jnp.concatenate([pre_grad, outer_grad], axis=0),
        )
        for k, v in enumerate((pre_grad.astype(F32), outer_grad.astype(F32), grad * normal, grad)):
            sums[k] += lane_sums(v)
        return pre_grad

    def backward_step(k):
        plane = plane_at(k)

        def two(ts):
            tos = [lax.rem(r + t + 1, ring) for t in ts]
            froms = [plane * ring + to for to in tos]
            both = gather_columns(
                tabs[1, z], side_by_side([receivers[a] for a in froms]), rows
            )
            for i, (t, to, a) in enumerate(zip(ts, tos, froms)):
                got = both[:, i * cap : (i + 1) * cap]

                @pl.when(k == 0)
                def _():
                    hand_over(1, z, to, t + 1, got, recv_c)

                send_d[a] = edge_backward(a, got)

        in_pairs(two)

    def send_back(k, low, high):
        loop(low, high, lambda t: back_copy(order[k] * ring + lax.rem(r + t, ring)).start())

    def emit(plan, slot, send):
        for k, q in plan.get(slot, ()):
            send(k, q * ring // 4, (q + 1) * ring // 4)

    def emit_at(plan, slot, turn, turns, send):
        for i in range(turns):
            if (slot, i) in plan:
                @pl.when(turn == i)
                def _():
                    emit(plan, (slot, i), send)

    for c in range(chunks):
        send_own(0, c)
    for k in range(1, PLANES):
        ids_copy(0, senders, k).start()
    load_edges.wait()
    send_edges(0, 1, ring)
    for j in range(owners):
        count_send[j] = jnp.full(count_send.shape[1:], counts[j], jnp.int32)
    peers(lambda j: count_copy(j).start())
    ids_tab[0, pl.ds(z * ring, ring)] = senders[pl.ds(z * ring, ring)]
    count_recv[e] = count_send[e]
    recv_e[e] = edges[:, lanes(e)]
    total[...] = jnp.zeros_like(total)
    grads[...] = jnp.zeros_like(grads)
    sums[...] = jnp.zeros_like(sums)

    def eye(n):
        return (
            lax.broadcasted_iota(jnp.int32, (n, n), 0) == lax.broadcasted_iota(jnp.int32, (n, n), 1)
        ).astype(F32).astype(BF16)

    unit = eye(rows)
    ew1[...] = dot_tn(ew1t[...], unit).astype(BF16)
    nw1[...] = dot_tn(nw1t[...], unit).astype(BF16)
    ew2t[...] = dot_tn(ew2[...], unit).astype(BF16)
    nw2t[...] = dot_tn(nw2[...], unit).astype(BF16)
    lines = [v[...].astype(F32)[None, :] for v in (eb1, eb2, eg, eh, nb1, nb2, ng, nh)]
    lines.append(masks[...].astype(F32))
    lines.append(jnp.zeros((-(8 + levels_count) % 16, rows), F32))
    cols[...] = dot_nt(unit, jnp.concatenate(lines, axis=0).astype(BF16))

    def forward_gathers(k):
        @pl.when(k == 1)
        def _():
            relay(0, 0)
            for other in range(1, PLANES):
                ids_arrival(0, order[other]).wait_recv()
            end_wait(0, 1)

        @pl.when(k == 2)
        def _():
            relay(0, 1)
            end_wait(0, 2)

        @pl.when(k == 3)
        def _():
            end_wait(0, 3)

        emit_at(EDGE_PLAN, "table", k, PLANES, send_edges)
        gather_step(0, k, recv_s)
        emit_at(EDGE_PLAN, "gather", k, PLANES, send_edges)

        def two(ts):
            js = [k * ring + t for t in ts]
            both = gather_columns(tabs[0, z], side_by_side([receivers[j] for j in js]), rows)
            for i, j in enumerate(js):
                mine[j] = both[:, i * cap : (i + 1) * cap]

        in_pairs(two)

    steps(forward_gathers)
    for k in range(1, PLANES):
        ids_copy(1, receivers, k).start()
    forward_steps()
    drain_planes(0, recv_s)

    load_target.wait()

    per = high_count // chunks
    wide = per * LOW
    node_first = jnp.zeros((2 * rows, rows), F32)
    node_second = jnp.zeros((rows, rows), F32)
    node_sums = [jnp.zeros((rows, 128), F32)] * 4
    for c in range(chunks):
        here = slice(c * wide, (c + 1) * wide)
        aggregate = jnp.concatenate(
            [total[h * rows : (h + 1) * rows, :] for h in range(c * per, (c + 1) * per)], axis=1
        ).astype(BF16)
        own = nodes[:, here]
        stacked = jnp.concatenate([own, aggregate], axis=0)
        pre, normal, inverse = branch_forward(
            nw1t[...], nw2t[...], column(cols, NB1), column(cols, NB2), stacked
        )
        gain = column(cols, NG)
        state = own.astype(F32) + (normal * gain + column(cols, NH))
        new_hold[:, here] = state.astype(BF16)
        weight = jnp.zeros((rows, wide), F32)
        for l in range(levels_count):
            weight = jnp.where(levels[:, here] == l, column(cols, CM + l), weight)
        weight = weight * land[:, here].astype(F32)
        grad = weight * (state - target[:, here].astype(F32))
        outer_grad, pre_grad, hidden = branch_backward(nw2[...], gain, grad, pre, normal, inverse)
        stacked_grad = dot(nw1[...], pre_grad)
        part[:, here] = grad + stacked_grad[:rows]
        low = stacked_grad[rows:].astype(BF16)
        for h in range(per):
            tabs[1, z, (c * per + h) * rows : (c * per + h + 1) * rows, :] = low[
                :, h * LOW : (h + 1) * LOW
            ]
        send_own(1, c)
        node_first = node_first + dot_nt(stacked, pre_grad)
        node_second = node_second + dot_nt(hidden, outer_grad)
        for k, v in enumerate((pre_grad.astype(F32), outer_grad.astype(F32), grad * normal, grad)):
            node_sums[k] = node_sums[k] + lane_sums(v)

    new_copy = pltpu.make_async_copy(new_hold, new_nodes, out_sem.at[0])
    new_copy.start()

    def backward_steps(k):
        backward_step(k)

        @pl.when(k == 0)
        def _():
            send_back(0, 1, ring)

        @pl.when(k == 1)
        def _():
            relay(1, 0)
            for other in range(1, PLANES):
                ids_arrival(1, order[other]).wait_recv()
            end_wait(1, 1)

        @pl.when(k == 2)
        def _():
            relay(1, 1)
            end_wait(1, 2)

        @pl.when(k == 3)
        def _():
            end_wait(1, 3)

        emit_at(BACK_PLAN, "table", k, PLANES, send_back)

        @pl.when(k > 0)
        def _():
            gather_step(1, k, recv_c)

        emit_at(BACK_PLAN, "gather", k, PLANES, send_back)

    steps(backward_steps)
    total[...] = jnp.zeros_like(total)

    def by_receiver(h):
        emit_at(BACK_PLAN, "sums", h, owners // 2, send_back)
        total[...] += scatter_columns(
            side_by_side([send_d[2 * h], send_d[2 * h + 1]]),
            side_by_side([receivers[2 * h], receivers[2 * h + 1]]), count,
        )

    loop(0, owners // 2, by_receiver)

    grads[: 2 * rows, rows:] = node_first
    grads[2 * rows : 3 * rows, rows:] = node_second
    grads[3 * rows :, :8] = jnp.concatenate(
        [sums[k].sum(axis=1, keepdims=True) for k in range(4)]
        + [v.sum(axis=1, keepdims=True) for v in node_sums],
        axis=1,
    )
    reducers = min(devices, grads.shape[0] // 8)
    height = grads.shape[0] // reducers

    def piece(d):
        return pl.ds(pl.multiple_of(d * height, 8), height)

    def piece_copy(d, device):
        return remote(
            grads.at[piece(d)], pieces.at[me], piece_send.at[d], piece_recv.at[me], device
        )

    def piece_arrival(d):
        return remote(
            grads.at[piece(0)], pieces.at[d], piece_send.at[0], piece_recv.at[d], (e, rep)
        )

    def sum_copy(d, device):
        return remote(
            summed.at[piece(me)], summed.at[piece(me)], sum_send.at[d], sum_recv.at[me], device
        )

    def sum_arrival(d):
        return remote(
            summed.at[piece(d)], summed.at[piece(d)], sum_send.at[0], sum_recv.at[d], (e, rep)
        )

    def to_reducers(body):
        def one(d, device):
            if reducers == devices:
                body(d, device)
            else:
                @pl.when(d < reducers)
                def _():
                    body(d, device)

        others(one)

    def as_reducer(body):
        if reducers == devices:
            body()
        else:
            pl.when(me < reducers)(body)

    to_reducers(lambda d, device: piece_copy(d, device).start())
    def node_total(w_rows):
        for h in range(high_count):
            here = slice(h * LOW, (h + 1) * LOW)
            part[:, here] += split_dot(ew1[w_rows, :], total[h * rows : (h + 1) * rows, :])

    node_total(slice(2 * rows, 3 * rows))
    total[...] = jnp.zeros_like(total)

    @as_reducer
    def _():
        pieces[me] = grads[piece(me), :]
        others(lambda d, device: piece_arrival(d).wait_recv())

        def add(d, running):
            return running + pieces[d]

        summed[piece(me), :] = lax.fori_loop(1, devices, add, pieces[0])
        others(lambda d, device: sum_copy(d, device).start())

    def grad_copy(j):
        return pltpu.make_async_copy(recv_c.at[j], edge_grad.at[:, lanes(j)], grad_sem.at[j])

    def finish_edges(j, pre_grad):
        grad = recv_c[j].astype(F32) * (place < counts[j]).astype(F32)
        recv_c[j] = (grad + dot(ew1[:rows, :], pre_grad)).astype(BF16)
        grad_copy(j).start()

    recv_d[e] = send_d[e]

    def finish(plane, ts, remotes):
        js = [plane * ring + lax.rem(r + ring - t, ring) for t in ts]
        for t, j, there in zip(ts, js, remotes):
            @pl.when(t > 0)
            def _():
                plane_arrival(1, j, recv_c).wait_recv()

            @pl.when(there)
            def _():
                back_arrival(j).wait_recv()

            finish_edges(j, recv_d[j])
        total[...] += scatter_columns(
            side_by_side([recv_d[j] for j in js]), side_by_side([senders[j] for j in js]), count
        )

    turns = PLANES * (ring // 2)
    step_in_pairs(finish, lambda i: emit_at(BACK_PLAN, "finish", i, turns, send_back))
    node_total(slice(rows, 2 * rows))
    node_hold[...] = part[...].astype(BF16)
    node_copy = pltpu.make_async_copy(node_hold, node_grad, out_sem.at[1])
    node_copy.start()

    drain_tables(0)
    drain_tables(1)
    drain_planes(1, recv_c)
    for k in range(1, PLANES):
        ids_copy(0, senders, k).wait_send()
        ids_copy(1, receivers, k).wait_send()
    peers(lambda j: count_copy(j).wait_send())
    peers(lambda j: edges_copy(j).wait_send())
    peers(lambda j: back_copy(j).wait_send())
    to_reducers(lambda d, device: piece_copy(d, device).wait_send())

    @as_reducer
    def _():
        others(lambda d, device: sum_copy(d, device).wait_send())

    to_reducers(lambda d, device: sum_arrival(d).wait_recv())
    loop(0, owners, lambda j: grad_copy(j).wait())
    new_copy.wait()
    node_copy.wait()


def layer(counts, nodes, edges, target, senders, receivers, levels, land, masks, *weights):
    rows, count = nodes.shape
    owners, _, cap = senders.shape
    slots = edges.shape[1]
    reps = lax.axis_size("rep")
    devices = owners * reps
    chunks = 4 if count // LOW % 4 == 0 else 1
    grad_shape = (4 * rows, 2 * rows)
    reducers = min(devices, grad_shape[0] // 8)
    blocks = (owners, rows, cap)
    dma = pltpu.SemaphoreType.DMA
    vmem = pl.BlockSpec(memory_space=pltpu.VMEM)
    stay = pl.BlockSpec(memory_space=pl.ANY)
    return pl.pallas_call(
        functools.partial(layer_kernel, masks.shape[0], reps),
        in_specs=[pl.BlockSpec(memory_space=pltpu.SMEM), vmem, stay, stay]
        + [vmem] * (5 + len(weights)),
        out_specs=[stay, stay, stay, vmem],
        out_shape=[
            jax.ShapeDtypeStruct((rows, count), BF16),
            jax.ShapeDtypeStruct((rows, count), BF16),
            jax.ShapeDtypeStruct((rows, slots), BF16),
            jax.ShapeDtypeStruct(grad_shape, F32),
        ],
        scratch_shapes=[
            pltpu.VMEM((rows, slots), BF16),
            pltpu.VMEM((rows, count), BF16),
            pltpu.VMEM((rows, count), BF16),
            pltpu.VMEM((rows, count), BF16),
            dma((2,)),
            dma((2,)),
            dma((owners,)),
            pltpu.VMEM((2, PLANES, rows * (count // LOW), LOW), BF16),
            pltpu.VMEM(blocks, BF16),
            pltpu.VMEM(blocks, BF16),
            pltpu.VMEM(blocks, BF16),
            pltpu.VMEM(blocks, BF16),
            pltpu.VMEM((2, owners, 1, cap), jnp.int32),
            pltpu.VMEM((owners, 1, 128), jnp.int32),
            pltpu.VMEM((owners, 1, 128), jnp.int32),
            pltpu.VMEM(blocks, F32),
            pltpu.VMEM(blocks, F32),
            pltpu.VMEM((owners, 1, cap), F32),
            pltpu.VMEM(blocks, BF16),
            pltpu.VMEM(blocks, BF16),
            pltpu.VMEM(blocks, BF16),
            pltpu.VMEM((rows * (count // LOW), LOW), F32),
            pltpu.VMEM((rows, count), F32),
            pltpu.VMEM(grad_shape, F32),
            pltpu.VMEM((4, rows, 128), F32),
            pltpu.VMEM((devices, grad_shape[0] // reducers, grad_shape[1]), F32),
            pltpu.VMEM((3 * rows, rows), BF16),
            pltpu.VMEM((rows, rows), BF16),
            pltpu.VMEM((2 * rows, rows), BF16),
            pltpu.VMEM((rows, rows), BF16),
            pltpu.VMEM((rows, 16 * -(-(8 + masks.shape[0]) // 16)), F32),
            dma((2, 5, chunks)),
            dma((2, PLANES, chunks)),
            dma((2, PLANES)),
            dma((2, PLANES)),
            dma((2, owners)),
            dma((2, owners)),
            dma((2, owners)),
            dma((2, owners)),
            dma((owners,)),
            dma((owners,)),
            dma((reducers,)),
            dma((devices,)),
            dma((devices,)),
            dma((reducers,)),
        ],
        compiler_params=pltpu.CompilerParams(
            vmem_limit_bytes=VMEM_LIMIT, collective_id=0, has_side_effects=True
        ),
        cost_estimate=pl.CostEstimate(
            flops=64 * 2**30, bytes_accessed=16 * 2**20, transcendentals=4 * 2**20
        ),
        name="layer",
    )(counts, nodes, edges, target, senders, receivers, levels, land, masks, *weights)


def hand_out_kernel(edge_in, new_in, node_in, packed, edge_grad, new_nodes, node_grad, *outs):
    edge_grad[...] = edge_in[...]
    new_nodes[...] = new_in[...]
    node_grad[...] = node_in[...]
    rows = packed.shape[1] // 2
    lines = packed[3 * rows :, :].T
    edge_first, edge_b1, edge_second, edge_b2, edge_g, edge_h = outs[:6]
    node_first, node_b1, node_second, node_b2, node_g, node_h = outs[6:]
    edge_first[...] = packed[: 3 * rows, :].T[:rows, :]
    edge_second[...] = packed[3 * rows :, rows:]
    node_first[...] = packed[: 2 * rows, :].T[rows:, :]
    node_second[...] = packed[2 * rows : 3 * rows, rows:]
    for k, out in enumerate((edge_b1, edge_b2, edge_g, edge_h, node_b1, node_b2, node_g, node_h)):
        out[...] = lines[k, :rows]


def hand_out(new_nodes, node_grad, edge_grad, packed):
    rows = packed.shape[1] // 2
    vmem = pl.BlockSpec(memory_space=pltpu.VMEM)
    shapes = [
        (rows, 3 * rows), (rows,), (rows, rows), (rows,), (rows,), (rows,),
        (rows, 2 * rows), (rows,), (rows, rows), (rows,), (rows,), (rows,),
    ]
    large = (edge_grad, new_nodes, node_grad)
    edge_grad, new_nodes, node_grad, *small = pl.pallas_call(
        hand_out_kernel,
        in_specs=[vmem] * 4,
        out_specs=[vmem] * (3 + len(shapes)),
        out_shape=[jax.ShapeDtypeStruct(a.shape, a.dtype) for a in large]
        + [jax.ShapeDtypeStruct(s, F32) for s in shapes],
        compiler_params=pltpu.CompilerParams(vmem_limit_bytes=VMEM_LIMIT),
        name="hand_out",
    )(*large, packed)
    small[0], small[6] = small[0].T, small[6].T
    return (new_nodes, node_grad, edge_grad, *small)


def per_device(
    nodes, edges, target, senders, receivers, counts, levels, land, channel_mask,
    edge_in, edge_in_bias, edge_out, edge_out_bias, edge_gain, edge_shift,
    node_in, node_in_bias, node_out, node_out_bias, node_gain, node_shift,
):
    count = nodes.shape[1]
    owners = lax.axis_size("edge")
    cap = edges.shape[1] // owners
    return hand_out(
        *layer(
            counts, nodes, edges, target,
            senders.reshape(owners, 1, cap), receivers.reshape(owners, 1, cap),
            levels.reshape(1, count), land.reshape(1, count), channel_mask,
            edge_in.T, edge_out, node_in.T, node_out,
            edge_in_bias, edge_out_bias, edge_gain, edge_shift,
            node_in_bias, node_out_bias, node_gain, node_shift,
        )
    )


def solution(mesh):
    over = ("edge", "rep")
    wide, line, same = P(None, over), P(over), P()
    return jax.shard_map(
        per_device,
        mesh=mesh,
        in_specs=(wide, wide, wide, line, line, line, line, line) + (same,) * 13,
        out_specs=(wide, wide, wide) + (same,) * 12,
        check_vma=False,
    )
```

profile of v0, /device:TPU:0, one launch (start us, length us, event | category | flops | bytes accessed | tf_op | source)
XLA Modules:
  0.0 176.9 jit_solution(9138924043466930188)
XLA Ops:
  0.7 172.3 %layer.1 = (bf16[64,4096]{1,0:T(8,128)(2,1)}, bf16[64,4096]{1,0:T(8,128)(2,1)}, bf16[64,16384]{1,0:T(8,128)(2,1)}, f32[256,128]{1,0:T(8,128)}) custom-call(s32[16]{0:T(128)} %counts.1, bf16[64,4096]{1,0:T(8,128)(2,1)} %nodes.1, bf16[64,16384]{1,0:T(8,128)(2,1)} %edges_in.1, bf16[64,4096]{1,0:T(8,128)(2,1)} %target_in.1, s32[16,1,1024]{2,1,0:T(1,128)} %bitcast.8, ...), custom_call_target="tpu_custom_call" | custom-call | flops 68719476736 | bytes 16777216 | tf_op jit(solution)/shard_map/layer/pallas_call | solution.py:735
  173.0 3.7 %hand_out.1 = (bf16[64,16384]{1,0:T(8,128)(2,1)}, bf16[64,4096]{1,0:T(8,128)(2,1)}, bf16[64,4096]{1,0:T(8,128)(2,1)}, f32[64,192]{1,0:T(8,128)}, f32[64]{0:T(128...) custom-call(bf16[64,16384]{1,0:T(8,128)(2,1)} %get-tuple-element.34., ...), custom_call_target="tpu_custom_call" | custom-call | tf_op jit(solution)/shard_map/hand_out/pallas_call | solution.py:827
where the time goes:
time: 177 us
  Pallas kernels  176 us (99%)
    pallas_call x1, Pallas kernels, layer(): pl.pallas_call(functools.partial(layer_kernel, masks.shape[0], reps), in_...  172 us
    pallas_call x1, Pallas kernels, hand_out(): pl.pallas_call(hand_out_kernel, in_specs=[vmem] * 4, out_specs=[vmem] * (...  3.75 us

commit v1 on v0

--- a/solution.py
+++ b/solution.py
@@ -1,4 +1,5 @@
 import functools
+import math
 
 import jax
 import jax.numpy as jnp
@@ -13,21 +14,24 @@
 LOW = 256
 VMEM_LIMIT = 60 * 2**20
 PLANES = 4
+LAG = 3
+TABLE_PARTS = 4
+NODE_PARTS = 4
 EDGE_PLAN = {
     ('table', 1): ((1, 0), (1, 1), (1, 2), (1, 3)),
     ('table', 2): ((2, 0), (2, 1), (2, 2), (2, 3)),
-    ('table', 3): ((3, 0),),
-    ('edges', 0): ((3, 1),),
+    ('edges', 0): ((3, 0),),
+    ('table', 3): ((3, 1),),
     ('edges', 2): ((3, 2),),
-    ('edges', 5): ((3, 3),),
+    ('edges', 4): ((3, 3),),
 }
 BACK_PLAN = {
     ('table', 1): ((1, 0), (1, 1), (1, 2), (1, 3)),
     ('table', 2): ((2, 0), (2, 1), (2, 2), (2, 3)),
     ('table', 3): ((3, 0),),
-    ('sums', 1): ((3, 1),),
-    ('sums', 7): ((3, 2),),
-    ('finish', 2): ((3, 3),),
+    ('gather', 3): ((3, 1),),
+    ('finish', 1): ((3, 2),),
+    ('finish', 3): ((3, 3),),
 }
 MESH = pl.DeviceIdType.MESH
 
@@ -131,17 +135,18 @@
     edges, target, new_hold, node_hold, in_sem, out_sem, grad_sem, tabs, send_a, recv_s, recv_e, mine, ids_tab, count_send, count_recv, pre_s, normal_s,
     inverse_s, recv_c, send_d, recv_d, total, part, grads, sums, pieces, ew1, ew2t, nw1, nw2t, cols,
     tab_send, tab_recv, ids_send, ids_recv, a_send, a_recv, b_send, b_recv, count_out, count_in,
-    piece_send, piece_recv, sum_send, sum_recv,
+    plane_sums, piece_send, piece_recv, plane_send, plane_recv, sum_send, sum_recv,
 ):
     rows, count = nodes.shape
-    owners, cap = senders.shape[0], senders.shape[2]
+    owners = count_send.shape[0]
+    cap = senders.shape[0] * senders.shape[1] // owners
+    lines_of = cap // senders.shape[1]
     ring = owners // PLANES
     high_count = count // LOW
     chunks = tab_recv.shape[2]
     chunk = tabs.shape[2] // chunks
     e, rep = lax.axis_index("edge"), lax.axis_index("rep")
     z, r = e // ring, e % ring
-    me, devices = e * reps + rep, owners * reps
     upper = z // 2
 
     def plane_at(k):
@@ -169,12 +174,17 @@
 
         lax.fori_loop(low, high, step, 0)
 
+    group, mine_of_group = ring * reps, r * reps + rep
+
+    def group_device(g):
+        return (z * ring + g // reps, lax.rem(g, reps))
+
     def others(body):
         def one(t):
-            d = lax.rem(me + t, devices)
-            body(d, (d // reps, lax.rem(d, reps)))
-
-        loop(1, devices, one)
+            g = lax.rem(mine_of_group + t, group)
+            body(g, group_device(g))
+
+        loop(1, group, one)
 
     load_edges = pltpu.make_async_copy(edges_in, edges, in_sem.at[0])
     load_target = pltpu.make_async_copy(target_in, target, in_sem.at[1])
@@ -182,14 +192,18 @@
     load_target.start()
 
     barrier = pltpu.get_barrier_semaphore()
-    others(
-        lambda d, device: pl.semaphore_signal(
-            barrier, inc=1, device_id=device, device_id_type=MESH
-        )
-    )
-
+
+    def greet(device):
+        pl.semaphore_signal(barrier, inc=1, device_id=device, device_id_type=MESH)
+
+    loop(1, owners, lambda t: greet((lax.rem(e + t, owners), rep)))
+
+    def greet_other_cores(t):
+        loop(0, ring, lambda place: greet((z * ring + place, lax.rem(rep + t, reps))))
+
+    loop(1, reps, greet_other_cores)
     stack_table(tabs.at[0, z], nodes[...])
-    pl.semaphore_wait(barrier, devices - 1)
+    pl.semaphore_wait(barrier, owners - 1 + ring * (reps - 1))
 
     def part_of(phase, plane, c):
         return tabs.at[phase, plane, pl.ds(c * chunk, chunk)]
@@ -212,10 +226,10 @@
         def _():
             table_copy(phase, z, c, 1, z - 1).start()
 
-    def relay(phase, slot):
+    def relay(phase, slot, low=0, high=None):
         @pl.when(middle)
         def _():
-            for c in range(chunks):
+            for c in range(low, chunks if high is None else high):
                 if slot == 0:
                     await_table(phase, z - toward, c)
                     table_copy(phase, z - toward, c, 2, z + toward).start()
@@ -247,15 +261,23 @@
                 table_copy(phase, z + toward, c, 3, z - toward).wait_send()
                 table_copy(phase, z + 2 * toward, c, 4, z - toward).wait_send()
 
+    def ids_rows(plane):
+        size = ring * lines_of
+        return pl.ds(pl.multiple_of(plane * size, size), size)
+
+    def ids_of(ids, j):
+        block = ids[pl.ds(pl.multiple_of(j * lines_of, lines_of), lines_of), :]
+        return side_by_side([block[i : i + 1] for i in range(lines_of)])
+
     def ids_copy(phase, ids, k):
         plane = lax.rem(z + k, PLANES)
         return remote(
-            ids.at[pl.ds(plane * ring, ring)], ids_tab.at[phase, pl.ds(z * ring, ring)],
+            ids.at[ids_rows(plane)], ids_tab.at[phase, ids_rows(z)],
             ids_send.at[phase, plane], ids_recv.at[phase, z], at(plane, r),
         )
 
     def ids_arrival(phase, plane):
-        rows_of = ids_tab.at[phase, pl.ds(plane * ring, ring)]
+        rows_of = ids_tab.at[phase, ids_rows(plane)]
         return remote(
             rows_of, rows_of, ids_send.at[phase, plane], ids_recv.at[phase, plane], at(plane, r)
         )
@@ -288,7 +310,7 @@
             tos = [lax.rem(r + t + 1, ring) for t in ts]
             got = gather_columns(
                 tabs[phase, plane],
-                side_by_side([ids_tab[phase, plane * ring + to] for to in tos]), rows,
+                side_by_side([ids_of(ids_tab.at[phase], plane * ring + to) for to in tos]), rows,
             )
             for i, (t, to) in enumerate(zip(ts, tos)):
                 hand_over(phase, plane, to, t + 1, got[:, i * cap : (i + 1) * cap], into)
@@ -338,17 +360,14 @@
     def in_pairs(body):
         loop(0, ring // 2, lambda h: body((2 * h, 2 * h + 1)))
 
-    def steps(body):
-        loop(0, PLANES, body)
-
-    def step_in_pairs(body, before):
-        def one(i):
-            k, h = i // (ring // 2), lax.rem(i, ring // 2)
+    def pairs_of(k, body):
+        half = ring // 2
+
+        def one(h):
             ts = (2 * h, 2 * h + 1)
-            before(i)
-            body(plane_at(k), ts, [k + t > 0 for t in ts])
-
-        loop(0, PLANES * (ring // 2), one)
+            body(k * half + h, plane_at(k), ts, [k + t > 0 for t in ts])
+
+        loop(0, half, one)
 
     def side_by_side(blocks):
         return jnp.concatenate(blocks, axis=1)
@@ -375,26 +394,25 @@
         updated = own.astype(F32) + (normal * column(cols, EG) + column(cols, EH))
         return (updated * live_here(a)).astype(BF16)
 
-    def forward_steps():
-        def two(plane, ts, remotes):
-            froms = [plane * ring + lax.rem(r + ring - t, ring) for t in ts]
-            for t, a, there in zip(ts, froms, remotes):
-                @pl.when(t > 0)
-                def _():
-                    plane_arrival(0, a, recv_s).wait_recv()
-
-                @pl.when(there)
-                def _():
-                    count_arrival(a).wait_recv()
-                    edges_arrival(a).wait_recv()
-
-            total[...] += scatter_columns(
-                side_by_side([edge_forward(a) for a in froms]),
-                side_by_side([receivers[a] for a in froms]), count,
-            )
-
-        turns = PLANES * (ring // 2)
-        step_in_pairs(two, lambda i: emit_at(EDGE_PLAN, "edges", i, turns, send_edges))
+    turns = PLANES * (ring // 2)
+
+    def forward_pair(turn, plane, ts, remotes):
+        emit_at(EDGE_PLAN, "edges", turn, turns, send_edges)
+        froms = [plane * ring + lax.rem(r + ring - t, ring) for t in ts]
+        for t, a, there in zip(ts, froms, remotes):
+            @pl.when(t > 0)
+            def _():
+                plane_arrival(0, a, recv_s).wait_recv()
+
+            @pl.when(there)
+            def _():
+                count_arrival(a).wait_recv()
+                edges_arrival(a).wait_recv()
+
+        total[...] += scatter_columns(
+            side_by_side([edge_forward(a) for a in froms]),
+            side_by_side([ids_of(receivers, a) for a in froms]), count,
+        )
 
     def edge_backward(a, got):
         grad = got.astype(F32) * live_here(a)
@@ -417,7 +435,7 @@
             tos = [lax.rem(r + t + 1, ring) for t in ts]
             froms = [plane * ring + to for to in tos]
             both = gather_columns(
-                tabs[1, z], side_by_side([receivers[a] for a in froms]), rows
+                tabs[1, z], side_by_side([ids_of(receivers, a) for a in froms]), rows
             )
             for i, (t, to, a) in enumerate(zip(ts, tos, froms)):
                 got = both[:, i * cap : (i + 1) * cap]
@@ -453,7 +471,9 @@
     for j in range(owners):
         count_send[j] = jnp.full(count_send.shape[1:], counts[j], jnp.int32)
     peers(lambda j: count_copy(j).start())
-    ids_tab[0, pl.ds(z * ring, ring)] = senders[pl.ds(z * ring, ring)]
+    for k in range(1, PLANES):
+        ids_copy(1, receivers, k).start()
+    ids_tab[0, ids_rows(z)] = senders[ids_rows(z)]
     count_recv[e] = count_send[e]
     recv_e[e] = edges[:, lanes(e)]
     total[...] = jnp.zeros_like(total)
@@ -497,27 +517,34 @@
         emit_at(EDGE_PLAN, "gather", k, PLANES, send_edges)
 
         def two(ts):
-            js = [k * ring + t for t in ts]
-            both = gather_columns(tabs[0, z], side_by_side([receivers[j] for j in js]), rows)
+            js = [plane_at(k) * ring + t for t in ts]
+            both = gather_columns(tabs[0, z], side_by_side([ids_of(receivers, j) for j in js]), rows)
             for i, j in enumerate(js):
                 mine[j] = both[:, i * cap : (i + 1) * cap]
 
         in_pairs(two)
 
-    steps(forward_gathers)
-    for k in range(1, PLANES):
-        ids_copy(1, receivers, k).start()
-    forward_steps()
+    def forward_steps(k):
+        @pl.when(k >= LAG)
+        def _():
+            pairs_of(k - LAG, forward_pair)
+
+        @pl.when(k < PLANES)
+        def _():
+            forward_gathers(k)
+
+    loop(0, PLANES + LAG, forward_steps)
     drain_planes(0, recv_s)
 
     load_target.wait()
 
-    per = high_count // chunks
+    node_parts = math.gcd(high_count, NODE_PARTS)
+    per = high_count // node_parts
     wide = per * LOW
     node_first = jnp.zeros((2 * rows, rows), F32)
     node_second = jnp.zeros((rows, rows), F32)
     node_sums = [jnp.zeros((rows, 128), F32)] * 4
-    for c in range(chunks):
+    for c in range(node_parts):
         here = slice(c * wide, (c + 1) * wide)
         aggregate = jnp.concatenate(
             [total[h * rows : (h + 1) * rows, :] for h in range(c * per, (c + 1) * per)], axis=1
@@ -543,7 +570,8 @@
             tabs[1, z, (c * per + h) * rows : (c * per + h + 1) * rows, :] = low[
                 :, h * LOW : (h + 1) * LOW
             ]
-        send_own(1, c)
+        for part_c in range(c * chunks // node_parts, (c + 1) * chunks // node_parts):
+            send_own(1, part_c)
         node_first = node_first + dot_nt(stacked, pre_grad)
         node_second = node_second + dot_nt(hidden, outer_grad)
         for k, v in enumerate((pre_grad.astype(F32), outer_grad.astype(F32), grad * normal, grad)):
@@ -571,29 +599,13 @@
             relay(1, 1)
             end_wait(1, 2)
 
-        @pl.when(k == 3)
-        def _():
-            end_wait(1, 3)
-
-        emit_at(BACK_PLAN, "table", k, PLANES, send_back)
-
-        @pl.when(k > 0)
-        def _():
+        @pl.when((k == 1) | (k == 2))
+        def _():
+            emit_at(BACK_PLAN, "table", k, PLANES, send_back)
             gather_step(1, k, recv_c)
-
-        emit_at(BACK_PLAN, "gather", k, PLANES, send_back)
-
-    steps(backward_steps)
-    total[...] = jnp.zeros_like(total)
-
-    def by_receiver(h):
-        emit_at(BACK_PLAN, "sums", h, owners // 2, send_back)
-        total[...] += scatter_columns(
-            side_by_side([send_d[2 * h], send_d[2 * h + 1]]),
-            side_by_side([receivers[2 * h], receivers[2 * h + 1]]), count,
-        )
-
-    loop(0, owners // 2, by_receiver)
+            emit_at(BACK_PLAN, "gather", k, PLANES, send_back)
+
+    loop(0, PLANES, backward_steps)
 
     grads[: 2 * rows, rows:] = node_first
     grads[2 * rows : 3 * rows, rows:] = node_second
@@ -602,68 +614,98 @@
         + [v.sum(axis=1, keepdims=True) for v in node_sums],
         axis=1,
     )
-    reducers = min(devices, grads.shape[0] // 8)
+    reducers = min(group, grads.shape[0] // 8)
     height = grads.shape[0] // reducers
 
-    def piece(d):
-        return pl.ds(pl.multiple_of(d * height, 8), height)
-
-    def piece_copy(d, device):
-        return remote(
-            grads.at[piece(d)], pieces.at[me], piece_send.at[d], piece_recv.at[me], device
-        )
-
-    def piece_arrival(d):
-        return remote(
-            grads.at[piece(0)], pieces.at[d], piece_send.at[0], piece_recv.at[d], (e, rep)
-        )
-
-    def sum_copy(d, device):
-        return remote(
-            summed.at[piece(me)], summed.at[piece(me)], sum_send.at[d], sum_recv.at[me], device
-        )
-
-    def sum_arrival(d):
-        return remote(
-            summed.at[piece(d)], summed.at[piece(d)], sum_send.at[0], sum_recv.at[d], (e, rep)
+    def piece(g):
+        return pl.ds(pl.multiple_of(g * height, 8), height)
+
+    def piece_copy(g, device):
+        return remote(
+            grads.at[piece(g)], pieces.at[mine_of_group],
+            piece_send.at[g], piece_recv.at[mine_of_group], device,
+        )
+
+    def piece_arrival(g):
+        return remote(
+            grads.at[piece(0)], pieces.at[g], piece_send.at[0], piece_recv.at[g], (e, rep)
+        )
+
+    def plane_sum_copy(k):
+        plane = lax.rem(z + k, PLANES)
+        return remote(
+            plane_sums.at[z], plane_sums.at[z], plane_send.at[plane], plane_recv.at[z],
+            at(plane, r),
+        )
+
+    def plane_sum_arrival(k):
+        plane = lax.rem(z + k, PLANES)
+        here = plane_sums.at[plane]
+        return remote(here, here, plane_send.at[plane], plane_recv.at[plane], (e, rep))
+
+    def sum_copy(g, device):
+        return remote(
+            summed.at[piece(mine_of_group)], summed.at[piece(mine_of_group)],
+            sum_send.at[g], sum_recv.at[mine_of_group], device,
+        )
+
+    def sum_arrival(g):
+        return remote(
+            summed.at[piece(g)], summed.at[piece(g)], sum_send.at[0], sum_recv.at[g], (e, rep)
         )
 
     def to_reducers(body):
-        def one(d, device):
-            if reducers == devices:
-                body(d, device)
+        def one(g, device):
+            if reducers == group:
+                body(g, device)
             else:
-                @pl.when(d < reducers)
+                @pl.when(g < reducers)
                 def _():
-                    body(d, device)
+                    body(g, device)
 
         others(one)
 
     def as_reducer(body):
-        if reducers == devices:
+        if reducers == group:
             body()
         else:
-            pl.when(me < reducers)(body)
-
-    to_reducers(lambda d, device: piece_copy(d, device).start())
+            pl.when(mine_of_group < reducers)(body)
+
+    to_reducers(lambda g, device: piece_copy(g, device).start())
+
+    total[...] = jnp.zeros_like(total)
+
+    def by_receiver(h):
+        emit_at(BACK_PLAN, "sums", h, owners // 2, send_back)
+        total[...] += scatter_columns(
+            side_by_side([send_d[2 * h], send_d[2 * h + 1]]),
+            side_by_side([ids_of(receivers, 2 * h), ids_of(receivers, 2 * h + 1)]), count,
+        )
+
+    loop(0, owners // 2, by_receiver)
+
     def node_total(w_rows):
-        for h in range(high_count):
-            here = slice(h * LOW, (h + 1) * LOW)
-            part[:, here] += split_dot(ew1[w_rows, :], total[h * rows : (h + 1) * rows, :])
+        sums_here = side_by_side([total[h * rows : (h + 1) * rows, :] for h in range(high_count)])
+        part[...] += split_dot(ew1[w_rows, :], sums_here)
 
     node_total(slice(2 * rows, 3 * rows))
     total[...] = jnp.zeros_like(total)
 
     @as_reducer
     def _():
-        pieces[me] = grads[piece(me), :]
-        others(lambda d, device: piece_arrival(d).wait_recv())
-
-        def add(d, running):
-            return running + pieces[d]
-
-        summed[piece(me), :] = lax.fori_loop(1, devices, add, pieces[0])
-        others(lambda d, device: sum_copy(d, device).start())
+        pieces[mine_of_group] = grads[piece(mine_of_group), :]
+        others(lambda g, device: piece_arrival(g).wait_recv())
+        running = pieces[0]
+        for g in range(1, group):
+            running = running + pieces[g]
+        plane_sums[z] = running
+        for k in range(1, PLANES):
+            plane_sum_copy(k).start()
+
+    end_wait(1, 3)
+    emit_at(BACK_PLAN, "table", PLANES - 1, PLANES, send_back)
+    gather_step(1, PLANES - 1, recv_c)
+    emit_at(BACK_PLAN, "gather", PLANES - 1, PLANES, send_back)
 
     def grad_copy(j):
         return pltpu.make_async_copy(recv_c.at[j], edge_grad.at[:, lanes(j)], grad_sem.at[j])
@@ -675,7 +717,8 @@
 
     recv_d[e] = send_d[e]
 
-    def finish(plane, ts, remotes):
+    def finish(turn, plane, ts, remotes):
+        emit_at(BACK_PLAN, "finish", turn, turns, send_back)
         js = [plane * ring + lax.rem(r + ring - t, ring) for t in ts]
         for t, j, there in zip(ts, js, remotes):
             @pl.when(t > 0)
@@ -688,11 +731,25 @@
 
             finish_edges(j, recv_d[j])
         total[...] += scatter_columns(
-            side_by_side([recv_d[j] for j in js]), side_by_side([senders[j] for j in js]), count
-        )
-
-    turns = PLANES * (ring // 2)
-    step_in_pairs(finish, lambda i: emit_at(BACK_PLAN, "finish", i, turns, send_back))
+            side_by_side([recv_d[j] for j in js]), side_by_side([ids_of(senders, j) for j in js]), count
+        )
+
+    def finish_step(k):
+        @pl.when(k == 2)
+        def _():
+            @as_reducer
+            def _():
+                for other in range(1, PLANES):
+                    plane_sum_arrival(other).wait_recv()
+                running = plane_sums[0]
+                for plane in range(1, PLANES):
+                    running = running + plane_sums[plane]
+                summed[piece(mine_of_group), :] = running
+                others(lambda g, device: sum_copy(g, device).start())
+
+        pairs_of(k, finish)
+
+    loop(0, PLANES, finish_step)
     node_total(slice(rows, 2 * rows))
     node_hold[...] = part[...].astype(BF16)
     node_copy = pltpu.make_async_copy(node_hold, node_grad, out_sem.at[1])
@@ -707,13 +764,15 @@
     peers(lambda j: count_copy(j).wait_send())
     peers(lambda j: edges_copy(j).wait_send())
     peers(lambda j: back_copy(j).wait_send())
-    to_reducers(lambda d, device: piece_copy(d, device).wait_send())
+    to_reducers(lambda g, device: piece_copy(g, device).wait_send())
 
     @as_reducer
     def _():
-        others(lambda d, device: sum_copy(d, device).wait_send())
-
-    to_reducers(lambda d, device: sum_arrival(d).wait_recv())
+        for k in range(1, PLANES):
+            plane_sum_copy(k).wait_send()
+        others(lambda g, device: sum_copy(g, device).wait_send())
+
+    to_reducers(lambda g, device: sum_arrival(g).wait_recv())
     loop(0, owners, lambda j: grad_copy(j).wait())
     new_copy.wait()
     node_copy.wait()
@@ -721,13 +780,14 @@
 
 def layer(counts, nodes, edges, target, senders, receivers, levels, land, masks, *weights):
     rows, count = nodes.shape
-    owners, _, cap = senders.shape
+    owners = lax.axis_size("edge")
     slots = edges.shape[1]
+    cap = slots // owners
     reps = lax.axis_size("rep")
-    devices = owners * reps
-    chunks = 4 if count // LOW % 4 == 0 else 1
+    group = owners // PLANES * reps
+    chunks = math.gcd(count // LOW, TABLE_PARTS)
     grad_shape = (4 * rows, 2 * rows)
-    reducers = min(devices, grad_shape[0] // 8)
+    reducers = min(group, grad_shape[0] // 8)
     blocks = (owners, rows, cap)
     dma = pltpu.SemaphoreType.DMA
     vmem = pl.BlockSpec(memory_space=pltpu.VMEM)
@@ -756,7 +816,7 @@
             pltpu.VMEM(blocks, BF16),
             pltpu.VMEM(blocks, BF16),
             pltpu.VMEM(blocks, BF16),
-            pltpu.VMEM((2, owners, 1, cap), jnp.int32),
+            pltpu.VMEM((2,) + senders.shape, jnp.int32),
             pltpu.VMEM((owners, 1, 128), jnp.int32),
             pltpu.VMEM((owners, 1, 128), jnp.int32),
             pltpu.VMEM(blocks, F32),
@@ -769,7 +829,7 @@
             pltpu.VMEM((rows, count), F32),
             pltpu.VMEM(grad_shape, F32),
             pltpu.VMEM((4, rows, 128), F32),
-            pltpu.VMEM((devices, grad_shape[0] // reducers, grad_shape[1]), F32),
+            pltpu.VMEM((group, grad_shape[0] // reducers, grad_shape[1]), F32),
             pltpu.VMEM((3 * rows, rows), BF16),
             pltpu.VMEM((rows, rows), BF16),
             pltpu.VMEM((2 * rows, rows), BF16),
@@ -785,10 +845,13 @@
             dma((2, owners)),
             dma((owners,)),
             dma((owners,)),
-            dma((reducers,)),
-            dma((devices,)),
-            dma((devices,)),
-            dma((reducers,)),
+            pltpu.VMEM((PLANES, grad_shape[0] // reducers, grad_shape[1]), F32),
+            dma((group,)),
+            dma((group,)),
+            dma((PLANES,)),
+            dma((PLANES,)),
+            dma((group,)),
+            dma((group,)),
         ],
         compiler_params=pltpu.CompilerParams(
             vmem_limit_bytes=VMEM_LIMIT, collective_id=0, has_side_effects=True
@@ -843,12 +906,10 @@
     node_in, node_in_bias, node_out, node_out_bias, node_gain, node_shift,
 ):
     count = nodes.shape[1]
-    owners = lax.axis_size("edge")
-    cap = edges.shape[1] // owners
     return hand_out(
         *layer(
             counts, nodes, edges, target,
-            senders.reshape(owners, 1, cap), receivers.reshape(owners, 1, cap),
+            senders.reshape(-1, 128), receivers.reshape(-1, 128),
             levels.reshape(1, count), land.reshape(1, count), channel_mask,
             edge_in.T, edge_out, node_in.T, node_out,
             edge_in_bias, edge_out_bias, edge_gain, edge_shift,

time: 177 us -> 171 us (0.966)
  Pallas kernels: 176 us -> 170 us
    pallas_call x1, Pallas kernels: 172 us -> 167 us  [layer(): pl.pallas_call(functools.partial(layer_kernel, masks.shape[0], reps), in_...]
where the time goes in v1:
time: 171 us
  Pallas kernels  170 us (99%)
    pallas_call x1, Pallas kernels, layer(): pl.pallas_call(functools.partial(layer_kernel, masks.shape[0], reps), in_...  167 us
    pallas_call x1, Pallas kernels, hand_out(): pl.pallas_call(hand_out_kernel, in_specs=[vmem] * 4, out_specs=[vmem] * (...  3.75 us

profile of v1, /device:TPU:0, one launch (start us, length us, event | category | flops | bytes accessed | tf_op | source)
XLA Modules:
  0.0 171.1 jit_solution(12408804768060632482)
XLA Ops:
  0.7 166.6 %layer.1 = (bf16[64,4096]{1,0:T(8,128)(2,1)}, bf16[64,4096]{1,0:T(8,128)(2,1)}, bf16[64,16384]{1,0:T(8,128)(2,1)}, f32[256,128]{1,0:T(8,128)}) custom-call(s32[16]{0:T(128)} %counts.1, bf16[64,4096]{1,0:T(8,128)(2,1)} %nodes.1, bf16[64,16384]{1,0:T(8,128)(2,1)} %edges_in.1, bf16[64,4096]{1,0:T(8,128)(2,1)} %target_in.1, s32[128,128]{1,0:T(8,128)} %bitcast.8, ...), custom_call_target="tpu_custom_call" | custom-call | flops 68719476736 | bytes 16777216 | tf_op jit(solution)/shard_map/layer/pallas_call | solution.py:795
  167.2 3.7 %hand_out.1 = (bf16[64,16384]{1,0:T(8,128)(2,1)}, bf16[64,4096]{1,0:T(8,128)(2,1)}, bf16[64,4096]{1,0:T(8,128)(2,1)}, f32[64,192]{1,0:T(8,128)}, f32[64]{0:T(128...) custom-call(bf16[64,16384]{1,0:T(8,128)(2,1)} %get-tuple-element.34., ...), custom_call_target="tpu_custom_call" | custom-call | tf_op jit(solution)/shard_map/hand_out/pallas_call | solution.py:890

commit v2 on v1

--- a/solution.py
+++ b/solution.py
@@ -14,24 +14,24 @@
 LOW = 256
 VMEM_LIMIT = 60 * 2**20
 PLANES = 4
-LAG = 3
 TABLE_PARTS = 4
 NODE_PARTS = 4
 EDGE_PLAN = {
-    ('table', 1): ((1, 0), (1, 1), (1, 2), (1, 3)),
-    ('table', 2): ((2, 0), (2, 1), (2, 2), (2, 3)),
-    ('edges', 0): ((3, 0),),
-    ('table', 3): ((3, 1),),
-    ('edges', 2): ((3, 2),),
-    ('edges', 4): ((3, 3),),
+    ('edges', 0): (((2, 0), (2, 1), (2, 2), (2, 3)), ()),
+    ('edges', 2): ((), ((3, 1),)),
+    ('edges', 3): (((3, 2),), ()),
+    ('edges', 4): ((), ((3, 3),)),
+    ('edges', 5): (((3, 3),), ((3, 2),)),
+    ('gather', 3): ((), ((3, 0),)),
+    ('table', 1): (((1, 0), (1, 1), (1, 2), (1, 3)), ((1, 0), (1, 1), (1, 2), (1, 3))),
+    ('table', 2): ((), ((2, 0), (2, 1), (2, 2), (2, 3))),
+    ('table', 3): (((3, 0), (3, 1)), ()),
 }
 BACK_PLAN = {
-    ('table', 1): ((1, 0), (1, 1), (1, 2), (1, 3)),
-    ('table', 2): ((2, 0), (2, 1), (2, 2), (2, 3)),
-    ('table', 3): ((3, 0),),
-    ('gather', 3): ((3, 1),),
-    ('finish', 1): ((3, 2),),
-    ('finish', 3): ((3, 3),),
+    ('sums', 6): (((3, 3),), ()),
+    ('table', 1): (((1, 0), (1, 1), (1, 2), (1, 3)), ((1, 0), (1, 1), (1, 2), (1, 3))),
+    ('table', 2): (((2, 0), (2, 1), (2, 2), (2, 3)), ((2, 0), (2, 1), (2, 2), (2, 3))),
+    ('table', 3): (((3, 0), (3, 1), (3, 2)), ((3, 0), (3, 1), (3, 2), (3, 3))),
 }
 MESH = pl.DeviceIdType.MESH
 
@@ -360,14 +360,15 @@
     def in_pairs(body):
         loop(0, ring // 2, lambda h: body((2 * h, 2 * h + 1)))
 
-    def pairs_of(k, body):
-        half = ring // 2
-
-        def one(h):
+    half = ring // 2
+
+    def turns_of(low, high, body):
+        def one(turn):
+            k, h = turn // half, lax.rem(turn, half)
             ts = (2 * h, 2 * h + 1)
-            body(k * half + h, plane_at(k), ts, [k + t > 0 for t in ts])
-
-        loop(0, half, one)
+            body(turn, plane_at(k), ts, [k + t > 0 for t in ts])
+
+        loop(low, high, one)
 
     def side_by_side(blocks):
         return jnp.concatenate(blocks, axis=1)
@@ -452,8 +453,18 @@
         loop(low, high, lambda t: back_copy(order[k] * ring + lax.rem(r + t, ring)).start())
 
     def emit(plan, slot, send):
-        for k, q in plan.get(slot, ()):
-            send(k, q * ring // 4, (q + 1) * ring // 4)
+        for body_at, parts in zip((at_ends, at_middle), plan.get(slot, ((), ()))):
+            if parts:
+                @body_at
+                def _():
+                    for k, q in parts:
+                        send(k, q * ring // 4, (q + 1) * ring // 4)
+
+    def at_ends(body):
+        pl.when(jnp.logical_not(middle))(body)
+
+    def at_middle(body):
+        pl.when(middle)(body)
 
     def emit_at(plan, slot, turn, turns, send):
         for i in range(turns):
@@ -516,24 +527,27 @@
         gather_step(0, k, recv_s)
         emit_at(EDGE_PLAN, "gather", k, PLANES, send_edges)
 
-        def two(ts):
-            js = [plane_at(k) * ring + t for t in ts]
+        def mine_pair(turn, plane, ts, _):
+            js = [plane * ring + t for t in ts]
             both = gather_columns(tabs[0, z], side_by_side([ids_of(receivers, j) for j in js]), rows)
             for i, j in enumerate(js):
                 mine[j] = both[:, i * cap : (i + 1) * cap]
 
-        in_pairs(two)
+        @pl.when(k < 3)
+        def _():
+            turns_of((k + k // 2) * half, (k + 1 + (k + 1) // 2) * half, mine_pair)
+
+    early = half * (2 - z * (3 - z) // 2)
 
     def forward_steps(k):
-        @pl.when(k >= LAG)
-        def _():
-            pairs_of(k - LAG, forward_pair)
+        last = k // PLANES
+        turns_of(last * early, k // 3 * early + last * (turns - early), forward_pair)
 
         @pl.when(k < PLANES)
         def _():
             forward_gathers(k)
 
-    loop(0, PLANES + LAG, forward_steps)
+    loop(0, PLANES + 1, forward_steps)
     drain_planes(0, recv_s)
 
     load_target.wait()
@@ -747,7 +761,7 @@
                 summed[piece(mine_of_group), :] = running
                 others(lambda g, device: sum_copy(g, device).start())
 
-        pairs_of(k, finish)
+        turns_of(k * half, (k + 1) * half, finish)
 
     loop(0, PLANES, finish_step)
     node_total(slice(rows, 2 * rows))

time: 171 us -> 166 us (0.971)
  Pallas kernels: 170 us -> 165 us
    pallas_call x1, Pallas kernels: 167 us -> 161 us  [layer(): pl.pallas_call(functools.partial(layer_kernel, masks.shape[0], reps), in_...]
where the time goes in v2:
time: 166 us
  Pallas kernels  165 us (99%)
    pallas_call x1, Pallas kernels, layer(): pl.pallas_call(functools.partial(layer_kernel, masks.shape[0], reps), in_...  161 us
    pallas_call x1, Pallas kernels, hand_out(): pl.pallas_call(hand_out_kernel, in_specs=[vmem] * 4, out_specs=[vmem] * (...  3.75 us

profile of v2, /device:TPU:0, one launch (start us, length us, event | category | flops | bytes accessed | tf_op | source)
XLA Modules:
  0.0 166.0 jit_solution(13228630190083603734)
XLA Ops:
  0.7 161.4 %layer.1 = (bf16[64,4096]{1,0:T(8,128)(2,1)}, bf16[64,4096]{1,0:T(8,128)(2,1)}, bf16[64,16384]{1,0:T(8,128)(2,1)}, f32[256,128]{1,0:T(8,128)}) custom-call(s32[16]{0:T(128)} %counts.1, bf16[64,4096]{1,0:T(8,128)(2,1)} %nodes.1, bf16[64,16384]{1,0:T(8,128)(2,1)} %edges_in.1, bf16[64,4096]{1,0:T(8,128)(2,1)} %target_in.1, s32[128,128]{1,0:T(8,128)} %bitcast.8, ...), custom_call_target="tpu_custom_call" | custom-call | flops 68719476736 | bytes 16777216 | tf_op jit(solution)/shard_map/layer/pallas_call | solution.py:809
  162.1 3.7 %hand_out.1 = (bf16[64,16384]{1,0:T(8,128)(2,1)}, bf16[64,4096]{1,0:T(8,128)(2,1)}, bf16[64,4096]{1,0:T(8,128)(2,1)}, f32[64,192]{1,0:T(8,128)}, f32[64]{0:T(128...) custom-call(bf16[64,16384]{1,0:T(8,128)(2,1)} %get-tuple-element.34., ...), custom_call_target="tpu_custom_call" | custom-call | tf_op jit(solution)/shard_map/hand_out/pallas_call | solution.py:904

commit v3 on v2

--- a/solution.py
+++ b/solution.py
@@ -17,7 +17,8 @@
 TABLE_PARTS = 4
 NODE_PARTS = 4
 EDGE_PLAN = {
-    ('edges', 0): (((2, 0), (2, 1), (2, 2), (2, 3)), ()),
+    ('edges', 0): (((2, 0), (2, 1)), ()),
+    ('edges', 1): (((2, 2), (2, 3)), ()),
     ('edges', 2): ((), ((3, 1),)),
     ('edges', 3): (((3, 2),), ()),
     ('edges', 4): ((), ((3, 3),)),
@@ -28,10 +29,11 @@
     ('table', 3): (((3, 0), (3, 1)), ()),
 }
 BACK_PLAN = {
+    ('finish', 1): (((3, 2),), ()),
     ('sums', 6): (((3, 3),), ()),
     ('table', 1): (((1, 0), (1, 1), (1, 2), (1, 3)), ((1, 0), (1, 1), (1, 2), (1, 3))),
     ('table', 2): (((2, 0), (2, 1), (2, 2), (2, 3)), ((2, 0), (2, 1), (2, 2), (2, 3))),
-    ('table', 3): (((3, 0), (3, 1), (3, 2)), ((3, 0), (3, 1), (3, 2), (3, 3))),
+    ('table', 3): (((3, 0), (3, 1)), ((3, 0), (3, 1), (3, 2), (3, 3))),
 }
 MESH = pl.DeviceIdType.MESH
 
@@ -479,12 +481,11 @@
         ids_copy(0, senders, k).start()
     load_edges.wait()
     send_edges(0, 1, ring)
-    for j in range(owners):
-        count_send[j] = jnp.full(count_send.shape[1:], counts[j], jnp.int32)
-    peers(lambda j: count_copy(j).start())
     for k in range(1, PLANES):
         ids_copy(1, receivers, k).start()
     ids_tab[0, ids_rows(z)] = senders[ids_rows(z)]
+    for j in range(owners):
+        count_send[j] = jnp.full(count_send.shape[1:], counts[j], jnp.int32)
     count_recv[e] = count_send[e]
     recv_e[e] = edges[:, lanes(e)]
     total[...] = jnp.zeros_like(total)
@@ -536,6 +537,8 @@
         @pl.when(k < 3)
         def _():
             turns_of((k + k // 2) * half, (k + 1 + (k + 1) // 2) * half, mine_pair)
+
+    peers(lambda j: count_copy(j).start())
 
     early = half * (2 - z * (3 - z) // 2)
 

time: 166 us -> 166 us (level)
  no operation moved by 1% of the time
where the time goes in v3:
time: 166 us
  Pallas kernels  165 us (99%)
    pallas_call x1, Pallas kernels, layer(): pl.pallas_call(functools.partial(layer_kernel, masks.shape[0], reps), in_...  161 us
    pallas_call x1, Pallas kernels, hand_out(): pl.pallas_call(hand_out_kernel, in_specs=[vmem] * 4, out_specs=[vmem] * (...  3.75 us

profile of v3, /device:TPU:0, one launch (start us, length us, event | category | flops | bytes accessed | tf_op | source)
XLA Modules:
  0.0 165.8 jit_solution(11300116189616122477)
XLA Ops:
  0.7 161.2 %layer.1 = (bf16[64,4096]{1,0:T(8,128)(2,1)}, bf16[64,4096]{1,0:T(8,128)(2,1)}, bf16[64,16384]{1,0:T(8,128)(2,1)}, f32[256,128]{1,0:T(8,128)}) custom-call(s32[16]{0:T(128)} %counts.1, bf16[64,4096]{1,0:T(8,128)(2,1)} %nodes.1, bf16[64,16384]{1,0:T(8,128)(2,1)} %edges_in.1, bf16[64,4096]{1,0:T(8,128)(2,1)} %target_in.1, s32[128,128]{1,0:T(8,128)} %bitcast.8, ...), custom_call_target="tpu_custom_call" | custom-call | flops 68719476736 | bytes 16777216 | tf_op jit(solution)/shard_map/layer/pallas_call | solution.py:812
  161.8 3.7 %hand_out.1 = (bf16[64,16384]{1,0:T(8,128)(2,1)}, bf16[64,4096]{1,0:T(8,128)(2,1)}, bf16[64,4096]{1,0:T(8,128)(2,1)}, f32[64,192]{1,0:T(8,128)}, f32[64]{0:T(128...) custom-call(bf16[64,16384]{1,0:T(8,128)(2,1)} %get-tuple-element.34., ...), custom_call_target="tpu_custom_call" | custom-call | tf_op jit(solution)/shard_map/hand_out/pallas_call | solution.py:907
